TPU v7x, 256 devices: a whole 4x4x8 slice. The times are simulated.
256 devices in a mesh: rows: 4 (over x), chan: 8 (over y, z_lo), filt: 8 (over z_hi, core).
Axes of the slice: x: 4, y: 4, z: 8 (z_hi: 4, z_lo: 2; z = z_hi * 2 + z_lo), core: 2. Of those that a mesh axis runs over, the one named last changes fastest.
Arguments:
- images: bfloat16 [16, 2048, 2048], P('rows', 'chan', 'filt'), may hold values from -6 to 6
- first_weight: bfloat16 [2048, 1024], P('chan', 'filt'), may hold values from -0.125 to 0.125
- group_weight: bfloat16 [3, 3, 32, 1024], P(None, None, None, 'filt'), may hold values from -0.375 to 0.375
- third_weight: bfloat16 [1024, 2048], P('chan', 'filt'), may hold values from -0.1875 to 0.1875
- out_grad: bfloat16 [16, 2048, 2048], P('rows', 'chan', 'filt'), may hold values from -6 to 6
Outputs:
- block_out: bfloat16 [16, 2048, 2048], P('rows', 'chan', 'filt')
- images_grad: float32 [16, 2048, 2048], P('rows', 'chan', 'filt')
- first_grad: float32 [2048, 1024], P('chan', 'filt')
- group_grad: float32 [3, 3, 32, 1024], P(None, None, None, 'filt')
- third_grad: float32 [1024, 2048], P('chan', 'filt')
All inputs are finite; a program needn't handle non-finite values.
Results may differ from a plain program's by a relative error of at most 0.006.
Values may be sent and summed in bfloat16 or wider, within the bound.
No kernel may reach another device: no remote copies, remote signals or barrier semaphores. Data moves between devices by JAX's collectives and lax.ppermute only.
A program may use at most 128 MiB of HBM per device.

v0:
```python
import jax
import jax.numpy as jnp
from jax import lax
from jax.sharding import PartitionSpec as P


def extended(block, sides, width):
    for axis, dim in sides:
        count = lax.axis_size(axis)
        forward = [(i, i + 1) for i in range(count - 1)]
        backward = [(target, source) for source, target in forward]
        low = lax.ppermute(
            lax.slice_in_dim(block, block.shape[dim] - width, None, axis=dim), axis, forward
        )
        high = lax.ppermute(lax.slice_in_dim(block, 0, width, axis=dim), axis, backward)
        block = jnp.concatenate([low, block, high], axis=dim)
    return block


def silu_slope(values):
    logistic = jax.nn.sigmoid(values)
    return logistic * (1.0 + values * (1.0 - logistic))


def group_conv(padded, kernel, groups_here):
    result = lax.conv_general_dilated(
        padded[None],
        kernel,
        (1, 1),
        "VALID",
        dimension_numbers=("NHWC", "HWIO", "NHWC"),
        feature_group_count=groups_here,
        preferred_element_type=jnp.float32,
    )
    return result[0]


def transposed_kernel(kernel, group_size, groups_here):
    pieces = kernel.reshape(3, 3, group_size, groups_here, group_size)
    swapped = jnp.transpose(pieces, (0, 1, 4, 3, 2)).reshape(
        3, 3, group_size, groups_here * group_size
    )
    return swapped[::-1, ::-1]


def kernel_partial(padded_first, group_delta, group_size, groups_here):
    rows_here = group_delta.shape[0]
    cols_here = group_delta.shape[1]
    pixels = rows_here * cols_here
    delta_groups = group_delta.reshape(pixels, groups_here, group_size)
    kernel_terms = []
    for row_shift in range(3):
        for col_shift in range(3):
            window = padded_first[
                row_shift : row_shift + rows_here, col_shift : col_shift + cols_here
            ]
            window = window.reshape(pixels, groups_here, group_size)
            kernel_terms.append(
                jnp.einsum("pgi,pgo->gio", window, delta_groups, preferred_element_type=jnp.float32)
            )
    kernel_part = jnp.stack(kernel_terms).reshape(3, 3, groups_here, group_size, group_size)
    kernel_part = jnp.transpose(kernel_part, (0, 1, 3, 2, 4))
    return kernel_part.reshape(3, 3, group_size, groups_here * group_size)


def body(images, first_weight, group_weight, third_weight, out_grad):
    rows_here = images.shape[0]
    cols_here = images.shape[1]
    group_size = group_weight.shape[2]
    first_panel, third_panel = (
        lax.all_gather(first_weight, "chan", axis=0, tiled=True),
        lax.all_gather(third_weight, "chan", axis=0, tiled=True),
    )
    pixels = rows_here * cols_here
    groups_here = group_weight.shape[3] // group_size
    gathered = lax.all_gather(images, "filt", axis=2, tiled=True)
    flat_images = gathered.reshape(pixels, gathered.shape[2])
    pre_first = jnp.dot(flat_images, first_panel, preferred_element_type=jnp.float32)
    act_first = (
        jax.nn.silu(pre_first)
        .astype(jnp.bfloat16)
        .reshape(rows_here, cols_here, first_panel.shape[1])
    )
    padded_first = extended(act_first, (("rows", 0), ("chan", 1)), 1)
    pre_group = group_conv(padded_first, group_weight, groups_here)
    act_group = jax.nn.silu(pre_group).astype(jnp.bfloat16)
    mid_whole = lax.all_gather(act_group, "filt", axis=2, tiled=True)
    flat_mid = mid_whole.reshape(pixels, mid_whole.shape[2])
    third_out = jnp.dot(flat_mid, third_panel, preferred_element_type=jnp.float32)
    own_images = images.reshape(pixels, images.shape[2]).astype(jnp.float32)
    block_out = (own_images + third_out).astype(jnp.bfloat16).reshape(images.shape)
    grad_flat = out_grad.reshape(pixels, out_grad.shape[2])
    mid_terms = lax.dot_general(
        grad_flat, third_panel, (((1,), (1,)), ((), ())), preferred_element_type=jnp.float32
    )
    mid_grad = lax.psum_scatter(
        mid_terms.reshape(rows_here, cols_here, mid_terms.shape[1]),
        "filt",
        scatter_dimension=2,
        tiled=True,
    )
    third_part = lax.dot_general(
        flat_mid, grad_flat, (((0,), (0,)), ((), ())), preferred_element_type=jnp.float32
    )
    group_delta = (mid_grad * silu_slope(pre_group)).astype(jnp.bfloat16)
    padded_delta = extended(group_delta, (("rows", 0), ("chan", 1)), 1)
    first_back = group_conv(
        padded_delta, transposed_kernel(group_weight, group_size, groups_here), groups_here
    )
    kernel_part = kernel_partial(padded_first, group_delta, group_size, groups_here)
    first_delta = (first_back.reshape(pixels, first_back.shape[2]) * silu_slope(pre_first)).astype(
        jnp.bfloat16
    )
    first_part = lax.dot_general(
        flat_images, first_delta, (((0,), (0,)), ((), ())), preferred_element_type=jnp.float32
    )
    input_terms = lax.dot_general(
        first_delta, first_panel, (((1,), (1,)), ((), ())), preferred_element_type=jnp.float32
    )
    back_images = lax.psum_scatter(
        input_terms.reshape(rows_here, cols_here, input_terms.shape[1]).astype(jnp.bfloat16),
        "filt",
        scatter_dimension=2,
        tiled=True,
    ).astype(jnp.float32)
    images_grad = out_grad.astype(jnp.float32) + back_images
    group_grad = lax.psum(kernel_part, ("rows", "chan"))
    first_total, third_total = lax.psum((first_part, third_part), "rows")
    first_grad, third_grad = (
        lax.psum_scatter(first_total, "chan", scatter_dimension=0, tiled=True),
        lax.psum_scatter(third_total, "chan", scatter_dimension=0, tiled=True),
    )
    return (block_out, images_grad, first_grad, group_grad, third_grad)


def solution(mesh):
    in_specs = (
        P("rows", "chan", "filt"),
        P("chan", "filt"),
        P(None, None, None, "filt"),
        P("chan", "filt"),
        P("rows", "chan", "filt"),
    )
    out_specs = (
        P("rows", "chan", "filt"),
        P("rows", "chan", "filt"),
        P("chan", "filt"),
        P(None, None, None, "filt"),
        P("chan", "filt"),
    )
    return jax.shard_map(body, mesh=mesh, in_specs=in_specs, out_specs=out_specs, check_vma=False)
```

profile of v0, /device:TPU:32, one launch (start us, length us, event | category | flops | bytes accessed | tf_op | source)
XLA Modules:
  0.0 700.0 jit_solution(2654013649618200023)
XLA Ops:
  7.9 39.6 %all_gather.15 = bf16[1024,256]{1,0:T(8,128)(2,1)S(1)} all-gather(bf16[128,256]{1,0:T(8,128)(2,1)} %param.8), channel_id=1, replica_groups=mesh['rows'=4,'chan'=8,'filt'=8] {'chan'}, dimensions={0}, use_global_device_ids=true | all-gather | bytes 589824 | tf_op jit(solution)/shard_map/all_gather | solution.py:72
  47.5 3.8 fusion.10
  52.2 36.9 %all_gather.13 = bf16[2048,128]{1,0:T(8,128)(2,1)S(1)} all-gather(bf16[256,128]{1,0:T(8,128)(2,1)S(1)} %copy-done.13), channel_id=1, replica_groups=mesh['rows'=4,'chan'=8,'filt'=8] {'chan'}, dimensions={0}, use_global_device_ids=true | all-gather | bytes 589824 | tf_op jit(solution)/shard_map/all_gather | solution.py:71
  89.1 4.4 multiply_convert_fusion.3
  93.5 2.9 collective-permute-start
  98.4 4.2 collective-permute-done.1
  103.2 3.4 collective-permute-start.2
  106.6 3.2 collective-permute-start.3
  110.7 8.0 %collective-permute-done.2 = bf16[6,1,128]{1,2,0:T(8,128)(2,1)S(1)} collective-permute-done((bf16[6,1,128]{1,2,0:T(8,128)(2,1)S(1)}, bf16[6,1,128]{1,2,0:T(8,128)(2,1)S(1)}, u32[]{:S(2)}, u32[]{:S(2)}) %collective-permute-start.2) | collective-permute-done | bytes 1568 | tf_op jit(solution)/shard_map/ppermute | solution.py:12
  118.7 10.6 %collective-permute-done.3 = bf16[6,1,128]{1,2,0:T(8,128)(2,1)S(1)} collective-permute-done((bf16[6,1,128]{1,2,0:T(8,128)(2,1)S(1)}, bf16[6,1,128]{1,2,0:T(8,128)(2,1)S(1)}, u32[]{:S(2)}, u32[]{:S(2)}) %collective-permute-start.3) | collective-permute-done | bytes 1568 | tf_op jit(solution)/shard_map/ppermute | solution.py:15
  130.0 5.8 copy.36
  135.8 9.4 %fusion.13 = f32[1,4,256,4,32]{4,0,3,2,1:T(1,128)S(1)} fusion(bf16[1,6,258,4,32]{4,0,3,2,1:T(2,128)(2,1)} %copy.36, bf16[3,3,32,4,32]{4,3,2,1,0:T(4,128)(2,1)} %shard_map.94), kind=kOutput, calls=%fused_computation.39 | convolution fusion | flops 75497472 | bytes 994304 | tf_op jit(solution)/shard_map/conv_general_dilated | solution.py:26
  145.3 3.5 copy.38
  150.2 2.0 multiply_convert_fusion.1
  152.2 3.3 collective-permute-start.4
  157.5 4.3 collective-permute-done.5
  161.8 3.5 collective-permute-start.6
  165.3 2.6 collective-permute-start.7
  169.2 2.5 collective-permute-done.7
  172.1 5.9 copy.44
  178.0 13.8 %convolution_reduce_fusion = f32[4,256,4,32]{3,2,1,0:T(4,128)S(1)} fusion(bf16[1,6,258,4,32]{4,0,3,2,1:T(2,128)(2,1)} %copy.44, bf16[3,3,32,4,32]{4,3,2,1,0:T(4,128)(2,1)} %rev.6), kind=kOutput, calls=%fused_computation.2 | convolution fusion | flops 75497472 | bytes 994304 | tf_op jit(solution)/shard_map/conv_general_dilated | solution.py:26
  194.9 4.0 convolution_bitcast_fusion
  199.0 3.4 convolution_bitcast_fusion.1
  202.4 40.0 %reduce-scatter.9.cloned.1.call-done = f32[256,128]{0,1:T(8,128)} async-done(((f32[2048,128]{0,1:T(8,128)}), f32[256,128]{0,1:T(8,128)}) %reduce-scatter.9.cloned.1.call-update) | async-done | bytes 131088 | tf_op jit(solution)/shard_map/reduce_scatter | solution.py:130
  242.4 44.5 %reduce-scatter.11.cloned.1.call-done = f32[128,256]{1,0:T(8,128)} async-done(((f32[1024,256]{1,0:T(8,128)}), f32[128,256]{1,0:T(8,128)}) %reduce-scatter.11.cloned.1.call-update) | async-done | bytes 131088 | tf_op jit(solution)/shard_map/reduce_scatter | solution.py:131
  286.9 3.2 convolution_convert_fusion
  294.3 1.8 reshape.85
  312.5 3.2 fusion
  315.6 21.3 %all-reduce.6.cloned.1.call-done = (f32[256,128]{0,1:T(8,128)}, f32[128,256]{1,0:T(8,128)}) async-done(((f32[256,128]{0,1:T(8,128)}, f32[128,256]{1,0:T(8,128)}), (f32[256,128]{0,1:T(8,128)}, f32[128,256]{1,0:T(8,128)})) %all-reduce.6.cloned.1.call-update) | async-done | bytes 262160 | tf_op jit(solution)/shard_map/psum | solution.py:128
  338.7 59.3 %reduce-scatter.7.cloned.1.call-done = bf16[4,256,256]{2,1,0:T(8,128)(2,1)} async-done(((bf16[4,256,2048]{2,1,0:T(8,128)(2,1)}), bf16[4,256,256]{2,1,0:T(8,128)(2,1)}) %reduce-scatter.7.cloned.1.call-update) | async-done | bytes 524304 | tf_op jit(solution)/shard_map/reduce_scatter | solution.py:120
  398.0 2.1 convert_add_fusion
  400.1 290.7 %all-reduce.4.cloned.1.call-done = f32[3,3,32,128]{3,2,1,0:T(8,128)} async-done(((f32[3,3,32,128]{3,2,1,0:T(8,128)}), f32[3,3,32,128]{3,2,1,0:T(8,128)}) %all-reduce.4.cloned.1.call-update) | async-done | bytes 147472 | tf_op jit(solution)/shard_map/psum | solution.py:127
  (106 shorter events, 38.3 us)
Async XLA Ops:
  7.2 81.9 %all-gather.3.cloned.1.call-start = ((), (), s32[]{:S(2)}) async-start(), calls=%async_computation.4 | async-start | bytes 4718592 | tf_op jit(solution)/shard_map/all_gather | solution.py:76
  7.9 142.2 %reduce-scatter.5.cloned.1.call-start = ((), (), s32[]{:S(2)}) async-start(), calls=%async_computation.6 | async-start | bytes 4718592 | tf_op jit(solution)/shard_map/reduce_scatter | solution.py:96
  51.3 0.8 copy-start.13
  51.4 147.6 %all-gather.5.cloned.1.call-start = ((), (), s32[]{:S(2)}) async-start(), calls=%async_computation.5 | async-start | bytes 2359296 | tf_op jit(solution)/shard_map/all_gather | solution.py:87
  89.1 4.4 copy-start
  93.5 16.3 %copy-start.12 = (bf16[3,3,32,128]{3,2,1,0:T(8,128)(2,1)S(1)}, bf16[3,3,32,128]{3,2,1,0:T(8,128)(2,1)}, u32[]{:S(2)}) copy-start(bf16[3,3,32,128]{3,2,1,0:T(8,128)(2,1)} %param.7) | copy-start | bytes 221188
  93.5 4.8 collective-permute-start
  96.4 6.2 collective-permute-start.1
  98.3 4.6 copy-start.7
  102.6 0.6 copy-start.9
  103.2 15.5 %collective-permute-start.2 = (bf16[6,1,128]{1,2,0:T(8,128)(2,1)S(1)}, bf16[6,1,128]{1,2,0:T(8,128)(2,1)S(1)}, u32[]{:S(2)}, u32[]{:S(2)}) collective-permute-start(bf16[6,1,128]{1,2,0:T(8,128)(2,1)S(1)} %get-tuple-element.29), channel_id=1, source_target_pairs={{0,8},{8,16},{16,24},{24,32},{32,40},{40,48},{48,56},{1,9},{9,17},... | collective-permute-start | bytes 4616 | tf_op jit(solution)/shard_map/ppermute | solution.py:12
  106.6 22.7 %collective-permute-start.3 = (bf16[6,1,128]{1,2,0:T(8,128)(2,1)S(1)}, bf16[6,1,128]{1,2,0:T(8,128)(2,1)S(1)}, u32[]{:S(2)}, u32[]{:S(2)}) collective-permute-start(bf16[6,1,128]{1,2,0:T(8,128)(2,1)S(1)} %get-tuple-element.30), channel_id=1, source_target_pairs={{8,0},{16,8},{24,16},{32,24},{40,32},{48,40},{56,48},{9,1},{17,9},... | collective-permute-start | bytes 4616 | tf_op jit(solution)/shard_map/ppermute | solution.py:15
  118.7 17.1 %copy-start.4 = (bf16[6,1,128]{1,2,0:T(8,128)(2,1)}, bf16[6,1,128]{1,2,0:T(8,128)(2,1)S(1)}, u32[]{:S(2)}) copy-start(bf16[6,1,128]{1,2,0:T(8,128)(2,1)S(1)} %collective-permute-done.2) | copy-start | bytes 4612
  129.3 0.7 copy-start.6
  148.8 19.0 %copy-start.3 = (bf16[3,3,32,4,32]{4,3,2,1,0:T(4,128)(2,1)S(1)}, bf16[3,3,32,4,32]{4,3,2,1,0:T(4,128)(2,1)}, u32[]{:S(2)}) copy-start(bf16[3,3,32,4,32]{4,3,2,1,0:T(4,128)(2,1)} %shard_map.94) | copy-start | bytes 221188
  152.2 90.2 %reduce-scatter.9.cloned.1.call-start = ((), (), s32[]{:S(2)}) async-start(), calls=%async_computation.9 | async-start | bytes 1179648 | tf_op jit(solution)/shard_map/reduce_scatter | solution.py:130
  152.2 5.2 collective-permute-start.4
  155.6 6.2 collective-permute-start.5
  161.8 7.4 %collective-permute-start.6 = (bf16[6,1,128]{2,1,0:T(2,128)(2,1)S(1)}, bf16[6,1,128]{2,1,0:T(2,128)(2,1)S(1)}, u32[]{:S(2)}, u32[]{:S(2)}) collective-permute-start(bf16[6,1,128]{2,1,0:T(2,128)(2,1)S(1)} %get-tuple-element.27), channel_id=1, source_target_pairs={{0,8},{8,16},{16,24},{24,32},{32,40},{40,48},{48,56},{1,9},{9,17},... | collective-permute-start | bytes 4616 | tf_op jit(solution)/shard_map/ppermute | solution.py:12
  165.3 6.4 collective-permute-start.7
  194.9 4.1 copy-start.2
  198.9 88.0 %copy-start.1 = (bf16[2048,128]{1,0:T(8,128)(2,1)S(1)}, bf16[2048,128]{1,0:T(8,128)(2,1)}, u32[]{:S(2)}) copy-start(bf16[2048,128]{1,0:T(8,128)(2,1)} %copy-done) | copy-start | bytes 1572868
  198.9 88.0 %reduce-scatter.11.cloned.1.call-start = ((), (), s32[]{:S(2)}) async-start(), calls=%async_computation.10 | async-start | bytes 1179648 | tf_op jit(solution)/shard_map/reduce_scatter | solution.py:131
  202.4 134.6 %all-reduce.6.cloned.1.call-start = ((), (), s32[]{:S(2)}) async-start(), calls=%async_computation.11 | async-start | bytes 524288 | tf_op jit(solution)/shard_map/psum | solution.py:128
  286.9 111.1 %reduce-scatter.7.cloned.1.call-start = ((), (), s32[]{:S(2)}) async-start(), calls=%async_computation.7 | async-start | bytes 4718592 | tf_op jit(solution)/shard_map/reduce_scatter | solution.py:120
  290.2 0.8 copy-start.8
  290.2 0.9 copy-start.10
  290.2 1.6 copy-start.5
  290.2 400.7 %all-reduce.4.cloned.1.call-start = ((), (), s32[]{:S(2)}) async-start(), calls=%async_computation.8 | async-start | bytes 294912 | tf_op jit(solution)/shard_map/psum | solution.py:127
  337.0 355.5 %copy-start.11 = (f32[128,256]{1,0:T(8,128)S(1)}, f32[128,256]{1,0:T(8,128)}, u32[]{:S(2)}) copy-start(f32[128,256]{1,0:T(8,128)} %get-tuple-element.46) | copy-start | bytes 393220
Sparse Core Ops, SparseCore 0:
  9.8 60.3 all-gather.2
  72.7 76.7 reduce-scatter.4
  152.3 42.8 all-gather.4
  199.0 43.3 reduce-scatter.8
  244.8 42.0 reduce-scatter.10
  289.1 47.8 all-reduce.5
  339.7 58.2 reduce-scatter.6
  401.4 289.4 all-reduce.3
where the time goes:
time: 701 us; the launch traced here: 700 us
  waiting for transfers between devices  487 us (69%)
  blocking collectives  76.5 us (11%)
  matrix products  49 us (7%)
  local copies, waits for them, and re-layouts  43.4 us (6%)
  starting transfers between devices  22 us (3%)
  between operations  14.5 us (2%)
  other arithmetic  7.29 us (1%)
    psum x1, waiting for transfers between devices, body(): group_grad = lax.psum(kernel_part, ('rows', 'chan'))  291 us
    reduce_scatter x1, waiting for transfers between devices, body(): lax.psum_scatter(input_terms.reshape(rows_here, cols_here, input_terms.sh...  59.3 us
    reduce_scatter x1, waiting for transfers between devices, body(): lax.psum_scatter(third_total, 'chan', scatter_dimension=0, tiled=True)  44.5 us
    reduce_scatter x1, waiting for transfers between devices, body(): lax.psum_scatter(first_total, 'chan', scatter_dimension=0, tiled=True)  40 us
    all_gather x1, blocking collectives, body(): lax.all_gather(third_weight, 'chan', axis=0, tiled=True)  39.6 us
    all_gather x1, blocking collectives, body(): lax.all_gather(first_weight, 'chan', axis=0, tiled=True)  36.9 us
    conv_general_dilated x2, matrix products, group_conv(): lax.conv_general_dilated(padded[None], kernel, (1, 1), 'VALID', dimension...  23.3 us
    ppermute x4, waiting for transfers between devices, extended(): lax.ppermute(lax.slice_in_dim(block, 0, width, axis=dim), axis, backward)  21.5 us
  transfers between devices with their start and end apart: 16, of which 12 were waited for; matrix products, arithmetic and copies ran while one was open for 13% of the time, Pallas kernels for 0%

commit v1 on v0

--- a/solution.py
+++ b/solution.py
@@ -124,7 +124,7 @@
         tiled=True,
     ).astype(jnp.float32)
     images_grad = out_grad.astype(jnp.float32) + back_images
-    group_grad = lax.psum(kernel_part, ("rows", "chan"))
+    group_grad = lax.psum(lax.psum(kernel_part, "chan"), "rows")
     first_total, third_total = lax.psum((first_part, third_part), "rows")
     first_grad, third_grad = (
         lax.psum_scatter(first_total, "chan", scatter_dimension=0, tiled=True),

time: 701 us -> 486 us (0.69)
  waiting for transfers between devices: 487 us -> 286 us
  local copies, waits for them, and re-layouts: 43.4 us -> 31.1 us
    psum x1, waiting for transfers between devices: 291 us -> 60.2 us  [body(): group_grad = lax.psum(lax.psum(kernel_part, 'chan'), 'rows')]
    psum x1, waiting for transfers between devices: 21.3 us -> 43.7 us  [body(): first_total, third_total = lax.psum((first_part, third_part), 'rows')]
  transfers between devices with their start and end apart: 16 -> 16, of which waited for: 12 -> 12; matrix products, arithmetic and copies ran while one was open for 13% -> 16% of each run, Pallas kernels for 0% -> 0%
where the time goes in v1:
time: 486 us; the launch traced here: 482 us
  waiting for transfers between devices  286 us (59%)
  blocking collectives  75.7 us (16%)
  matrix products  47 us (10%)
  local copies, waits for them, and re-layouts  31.1 us (6%)
  starting transfers between devices  22.6 us (5%)
  between operations  14.7 us (3%)
  other arithmetic  5.17 us (1%)
    psum x1, waiting for transfers between devices, body(): group_grad = lax.psum(lax.psum(kernel_part, 'chan'), 'rows')  60.2 us
    reduce_scatter x1, waiting for transfers between devices, body(): lax.psum_scatter(input_terms.reshape(rows_here, cols_here, input_terms.sh...  59.3 us
    reduce_scatter x1, waiting for transfers between devices, body(): lax.psum_scatter(first_total, 'chan', scatter_dimension=0, tiled=True)  45.2 us
    reduce_scatter x1, waiting for transfers between devices, body(): lax.psum_scatter(third_total, 'chan', scatter_dimension=0, tiled=True)  44.5 us
    psum x1, waiting for transfers between devices, body(): first_total, third_total = lax.psum((first_part, third_part), 'rows')  43.7 us
    all_gather x1, blocking collectives, body(): lax.all_gather(third_weight, 'chan', axis=0, tiled=True)  39.6 us
    all_gather x1, blocking collectives, body(): lax.all_gather(first_weight, 'chan', axis=0, tiled=True)  36.2 us
    conv_general_dilated x2, matrix products, group_conv(): lax.conv_general_dilated(padded[None], kernel, (1, 1), 'VALID', dimension...  23.2 us
  transfers between devices with their start and end apart: 16, of which 12 were waited for; matrix products, arithmetic and copies ran while one was open for 16% of the time, Pallas kernels for 0%

profile of v1, /device:TPU:32, one launch (start us, length us, event | category | flops | bytes accessed | tf_op | source)
XLA Modules:
  0.0 482.3 jit_solution(7897267235663076131)
XLA Ops:
  7.9 39.6 %all_gather.15 = bf16[1024,256]{1,0:T(8,128)(2,1)S(1)} all-gather(bf16[128,256]{1,0:T(8,128)(2,1)} %param.8), channel_id=1, replica_groups=mesh['rows'=4,'chan'=8,'filt'=8] {'chan'}, dimensions={0}, use_global_device_ids=true | all-gather | bytes 589824 | tf_op jit(solution)/shard_map/all_gather | solution.py:72
  48.3 3.8 fusion.10
  53.0 36.2 %all_gather.13 = bf16[2048,128]{1,0:T(8,128)(2,1)S(1)} all-gather(bf16[256,128]{1,0:T(8,128)(2,1)S(1)} %copy-done.21), channel_id=1, replica_groups=mesh['rows'=4,'chan'=8,'filt'=8] {'chan'}, dimensions={0}, use_global_device_ids=true | all-gather | bytes 589824 | tf_op jit(solution)/shard_map/all_gather | solution.py:71
  89.1 4.4 multiply_convert_fusion.3
  93.6 2.7 collective-permute-start
  98.2 4.2 collective-permute-done.1
  102.7 3.8 collective-permute-start.2
  106.5 3.1 collective-permute-start.3
  109.8 8.9 %collective-permute-done.2 = bf16[6,1,128]{1,2,0:T(8,128)(2,1)S(1)} collective-permute-done((bf16[6,1,128]{1,2,0:T(8,128)(2,1)S(1)}, bf16[6,1,128]{1,2,0:T(8,128)(2,1)S(1)}, u32[]{:S(2)}, u32[]{:S(2)}) %collective-permute-start.2) | collective-permute-done | bytes 1568 | tf_op jit(solution)/shard_map/ppermute | solution.py:12
  118.7 11.7 %collective-permute-done.3 = bf16[6,1,128]{1,2,0:T(8,128)(2,1)S(1)} collective-permute-done((bf16[6,1,128]{1,2,0:T(8,128)(2,1)S(1)}, bf16[6,1,128]{1,2,0:T(8,128)(2,1)S(1)}, u32[]{:S(2)}, u32[]{:S(2)}) %collective-permute-start.3) | collective-permute-done | bytes 1568 | tf_op jit(solution)/shard_map/ppermute | solution.py:15
  130.8 5.9 %copy.36 = bf16[1,6,258,4,32]{4,0,3,2,1:T(2,128)(2,1)} copy(bf16[1,6,258,4,32]{2,4,3,1,0:T(8,128)(2,1)S(1)} %bitcast.121) | data formatting | bytes 792576 | tf_op jit(solution)/shard_map/broadcast_in_dim | solution.py:27
  136.7 9.4 %fusion.13 = f32[1,4,256,4,32]{4,0,3,2,1:T(1,128)S(1)} fusion(bf16[1,6,258,4,32]{4,0,3,2,1:T(2,128)(2,1)} %copy.36, bf16[3,3,32,4,32]{4,3,2,1,0:T(4,128)(2,1)S(1)} %shard_map.94), kind=kOutput, calls=%fused_computation.39 | convolution fusion | flops 75497472 | bytes 994304 | tf_op jit(solution)/shard_map/conv_general_dilated | solution.py:26
  149.2 2.0 multiply_convert_fusion.1
  157.2 3.9 collective-permute-start.4
  164.0 3.2 collective-permute-done.5
  167.2 3.9 collective-permute-start.6
  171.2 1.9 collective-permute-start.7
  175.0 2.6 collective-permute-done.7
  178.7 6.9 %copy.44 = bf16[1,6,258,4,32]{4,0,3,2,1:T(2,128)(2,1)S(1)} copy(bf16[1,6,258,4,32]{2,4,3,1,0:T(8,128)(2,1)} %bitcast.120) | data formatting | bytes 792576 | tf_op jit(solution)/shard_map/broadcast_in_dim | solution.py:27
  185.7 13.8 %convolution_reduce_fusion = f32[4,256,4,32]{3,2,1,0:T(4,128)} fusion(bf16[1,6,258,4,32]{4,0,3,2,1:T(2,128)(2,1)S(1)} %copy.44, bf16[3,3,32,4,32]{4,3,2,1,0:T(4,128)(2,1)S(1)} %copy-done.13), kind=kOutput, calls=%fused_computation.2 | convolution fusion | flops 75497472 | bytes 994304 | tf_op jit(solution)/shard_map/conv_general_dilated | solution.py:26
  199.5 2.5 reshape.99
  202.2 4.0 convolution_bitcast_fusion
  206.3 3.4 convolution_bitcast_fusion.1
  209.8 60.2 %all-reduce.4.cloned.1.call-done = f32[3,3,32,128]{3,2,1,0:T(8,128)} async-done(((f32[3,3,32,128]{3,2,1,0:T(8,128)}), f32[3,3,32,128]{3,2,1,0:T(8,128)}) %all-reduce.4.cloned.1.call-update) | async-done | bytes 147472 | tf_op jit(solution)/shard_map/psum | solution.py:127
  270.0 45.2 %reduce-scatter.9.cloned.1.call-done = f32[256,128]{0,1:T(8,128)} async-done(((f32[2048,128]{0,1:T(8,128)}), f32[256,128]{0,1:T(8,128)}) %reduce-scatter.9.cloned.1.call-update) | async-done | bytes 131088 | tf_op jit(solution)/shard_map/reduce_scatter | solution.py:130
  315.2 44.5 %reduce-scatter.11.cloned.1.call-done = f32[128,256]{1,0:T(8,128)} async-done(((f32[1024,256]{1,0:T(8,128)}), f32[128,256]{1,0:T(8,128)}) %reduce-scatter.11.cloned.1.call-update) | async-done | bytes 131088 | tf_op jit(solution)/shard_map/reduce_scatter | solution.py:131
  359.8 3.2 convolution_convert_fusion
  364.2 3.1 fusion
  367.3 43.7 %all-reduce.6.cloned.1.call-done = (f32[256,128]{0,1:T(8,128)}, f32[3,3,32,128]{3,2,1,0:T(8,128)}, f32[128,256]{1,0:T(8,128)}) async-done(((f32[256,128]{0,1:T(8,128)}, f32[3,3,32,128]{3,2,1,0:T(8,128)}, f32[128,256]{1,0:T(8,128)}), (f32[256,128]{0,1:T(8,128)}, f32[3,3,32,128]{3,2,1,0:T(8,128)}, f32[128,256]{1,0:T(8,128)})) %all-reduce.6.cloned.1.call-update) | async-done | bytes 409616 | tf_op jit(solution)/shard_map/psum | solution.py:128
  411.0 1.7 copy.60
  412.7 59.3 %reduce-scatter.7.cloned.1.call-done = bf16[4,256,256]{2,1,0:T(8,128)(2,1)} async-done(((bf16[4,256,2048]{2,1,0:T(8,128)(2,1)}), bf16[4,256,256]{2,1,0:T(8,128)(2,1)}) %reduce-scatter.7.cloned.1.call-update) | async-done | bytes 524304 | tf_op jit(solution)/shard_map/reduce_scatter | solution.py:120
  472.0 2.1 convert_add_fusion
  (122 shorter events, 22.9 us)
Async XLA Ops:
  7.2 82.0 %all-gather.3.cloned.1.call-start = ((), (), s32[]{:S(2)}) async-start(), calls=%async_computation.4 | async-start | bytes 4718592 | tf_op jit(solution)/shard_map/all_gather | solution.py:76
  7.9 141.3 %reduce-scatter.5.cloned.1.call-start = ((), (), s32[]{:S(2)}) async-start(), calls=%async_computation.6 | async-start | bytes 4718592 | tf_op jit(solution)/shard_map/reduce_scatter | solution.py:96
  52.2 154.1 %all-gather.5.cloned.1.call-start = ((), (), s32[]{:S(2)}) async-start(), calls=%async_computation.5 | async-start | bytes 2359296 | tf_op jit(solution)/shard_map/all_gather | solution.py:87
  89.1 4.4 copy-start.2
  93.6 16.0 %copy-start.20 = (bf16[3,3,32,128]{3,2,1,0:T(8,128)(2,1)S(1)}, bf16[3,3,32,128]{3,2,1,0:T(8,128)(2,1)}, u32[]{:S(2)}) copy-start(bf16[3,3,32,128]{3,2,1,0:T(8,128)(2,1)} %param.7) | copy-start | bytes 221188
  93.6 4.5 collective-permute-start
  96.2 6.2 %collective-permute-start.1 = (bf16[1,256,128]{2,1,0:T(8,128)(2,1)S(1)}, bf16[1,256,128]{2,1,0:T(8,128)(2,1)S(1)}, u32[]{:S(2)}, u32[]{:S(2)}) collective-permute-start(bf16[1,256,128]{2,1,0:T(8,128)(2,1)S(1)} %get-tuple-element.37), channel_id=1, source_target_pairs={{64,0},{128,64},{192,128},{65,1},{129,65},{193,129},{66,2},{130,66... | collective-permute-start | bytes 196616 | tf_op jit(solution)/shard_map/ppermute | solution.py:15
  98.1 8.4 %copy-start.14 = (bf16[1,256,128]{2,1,0:T(8,128)(2,1)}, bf16[1,256,128]{2,1,0:T(8,128)(2,1)S(1)}, u32[]{:S(2)}) copy-start(bf16[1,256,128]{2,1,0:T(8,128)(2,1)S(1)} %collective-permute-done) | copy-start | bytes 196612
  102.4 4.1 copy-start.16
  102.7 16.0 %collective-permute-start.2 = (bf16[6,1,128]{1,2,0:T(8,128)(2,1)S(1)}, bf16[6,1,128]{1,2,0:T(8,128)(2,1)S(1)}, u32[]{:S(2)}, u32[]{:S(2)}) collective-permute-start(bf16[6,1,128]{1,2,0:T(8,128)(2,1)S(1)} %get-tuple-element.30), channel_id=1, source_target_pairs={{0,8},{8,16},{16,24},{24,32},{32,40},{40,48},{48,56},{1,9},{9,17},... | collective-permute-start | bytes 4616 | tf_op jit(solution)/shard_map/ppermute | solution.py:12
  106.5 23.9 %collective-permute-start.3 = (bf16[6,1,128]{1,2,0:T(8,128)(2,1)S(1)}, bf16[6,1,128]{1,2,0:T(8,128)(2,1)S(1)}, u32[]{:S(2)}, u32[]{:S(2)}) collective-permute-start(bf16[6,1,128]{1,2,0:T(8,128)(2,1)S(1)} %get-tuple-element.31), channel_id=1, source_target_pairs={{8,0},{16,8},{24,16},{32,24},{40,32},{48,40},{56,48},{9,1},{17,9},... | collective-permute-start | bytes 4616 | tf_op jit(solution)/shard_map/ppermute | solution.py:15
  109.8 26.9 %copy-start.5 = (bf16[3,3,32,4,32]{4,3,2,1,0:T(4,128)(2,1)}, bf16[3,3,32,4,32]{4,3,2,1,0:T(4,128)(2,1)S(1)}, u32[]{:S(2)}) copy-start(bf16[3,3,32,4,32]{4,3,2,1,0:T(4,128)(2,1)S(1)} %shard_map.94) | copy-start | bytes 221188
  118.7 18.0 %copy-start.7 = (bf16[6,1,128]{1,2,0:T(8,128)(2,1)}, bf16[6,1,128]{1,2,0:T(8,128)(2,1)S(1)}, u32[]{:S(2)}) copy-start(bf16[6,1,128]{1,2,0:T(8,128)(2,1)S(1)} %collective-permute-done.2) | copy-start | bytes 4612
  130.5 6.2 %copy-start.9 = (bf16[6,1,128]{1,2,0:T(8,128)(2,1)}, bf16[6,1,128]{1,2,0:T(8,128)(2,1)S(1)}, u32[]{:S(2)}) copy-start(bf16[6,1,128]{1,2,0:T(8,128)(2,1)S(1)} %collective-permute-done.3) | copy-start | bytes 4612
  147.7 3.8 copy-start.6
  147.9 5.1 %copy-start.15 = (bf16[1,256,128]{2,1,0:T(8,128)(2,1)S(1)}, bf16[1,256,128]{2,1,0:T(8,128)(2,1)}, u32[]{:S(2)}) copy-start(bf16[1,256,128]{2,1,0:T(8,128)(2,1)} %copy-done.14) | copy-start | bytes 196612
  147.9 5.1 %copy-start.17 = (bf16[1,256,128]{2,1,0:T(8,128)(2,1)S(1)}, bf16[1,256,128]{2,1,0:T(8,128)(2,1)}, u32[]{:S(2)}) copy-start(bf16[1,256,128]{2,1,0:T(8,128)(2,1)} %copy-done.16) | copy-start | bytes 196612
  151.2 118.8 %all-reduce.4.cloned.1.call-start = ((), (), s32[]{:S(2)}) async-start(), calls=%async_computation.8 | async-start | bytes 294912 | tf_op jit(solution)/shard_map/psum | solution.py:127
  157.2 6.8 %collective-permute-start.4 = (bf16[1,256,128]{2,1,0:T(8,128)(2,1)S(1)}, bf16[1,256,128]{2,1,0:T(8,128)(2,1)S(1)}, u32[]{:S(2)}, u32[]{:S(2)}) collective-permute-start(bf16[1,256,128]{2,1,0:T(8,128)(2,1)S(1)} %get-tuple-element.34), channel_id=1, source_target_pairs={{0,64},{64,128},{128,192},{1,65},{65,129},{129,193},{2,66},{66,130... | collective-permute-start | bytes 196616 | tf_op jit(solution)/shard_map/ppermute | solution.py:12
  161.1 6.2 %collective-permute-start.5 = (bf16[1,256,128]{2,1,0:T(8,128)(2,1)S(1)}, bf16[1,256,128]{2,1,0:T(8,128)(2,1)S(1)}, u32[]{:S(2)}, u32[]{:S(2)}) collective-permute-start(bf16[1,256,128]{2,1,0:T(8,128)(2,1)S(1)} %get-tuple-element.35), channel_id=1, source_target_pairs={{64,0},{128,64},{192,128},{65,1},{129,65},{193,129},{66,2},{130,66... | collective-permute-start | bytes 196616 | tf_op jit(solution)/shard_map/ppermute | solution.py:15
  167.2 7.8 %collective-permute-start.6 = (bf16[6,1,128]{2,1,0:T(2,128)(2,1)S(1)}, bf16[6,1,128]{2,1,0:T(2,128)(2,1)S(1)}, u32[]{:S(2)}, u32[]{:S(2)}) collective-permute-start(bf16[6,1,128]{2,1,0:T(2,128)(2,1)S(1)} %get-tuple-element.28), channel_id=1, source_target_pairs={{0,8},{8,16},{16,24},{24,32},{32,40},{40,48},{48,56},{1,9},{9,17},... | collective-permute-start | bytes 4616 | tf_op jit(solution)/shard_map/ppermute | solution.py:12
  171.2 6.4 %collective-permute-start.7 = (bf16[6,1,128]{2,1,0:T(2,128)(2,1)S(1)}, bf16[6,1,128]{2,1,0:T(2,128)(2,1)S(1)}, u32[]{:S(2)}, u32[]{:S(2)}) collective-permute-start(bf16[6,1,128]{2,1,0:T(2,128)(2,1)S(1)} %get-tuple-element.29), channel_id=1, source_target_pairs={{8,0},{16,8},{24,16},{32,24},{40,32},{48,40},{56,48},{9,1},{17,9},... | collective-permute-start | bytes 4616 | tf_op jit(solution)/shard_map/ppermute | solution.py:15
  174.7 140.5 %reduce-scatter.9.cloned.1.call-start = ((), (), s32[]{:S(2)}) async-start(), calls=%async_computation.9 | async-start | bytes 1179648 | tf_op jit(solution)/shard_map/reduce_scatter | solution.py:130
  178.7 6.9 %copy-start.13 = (bf16[3,3,32,4,32]{4,3,2,1,0:T(4,128)(2,1)S(1)}, bf16[3,3,32,4,32]{4,3,2,1,0:T(4,128)(2,1)}, u32[]{:S(2)}) copy-start(bf16[3,3,32,4,32]{4,3,2,1,0:T(4,128)(2,1)} %rev.6) | copy-start | bytes 221188
  199.5 2.5 copy-start.12
  202.2 4.1 copy-start.4
  206.2 153.6 %copy-start.3 = (bf16[2048,128]{1,0:T(8,128)(2,1)S(1)}, bf16[2048,128]{1,0:T(8,128)(2,1)}, u32[]{:S(2)}) copy-start(bf16[2048,128]{1,0:T(8,128)(2,1)} %copy-done.2) | copy-start | bytes 1572868
  206.2 153.5 %reduce-scatter.11.cloned.1.call-start = ((), (), s32[]{:S(2)}) async-start(), calls=%async_computation.10 | async-start | bytes 1179648 | tf_op jit(solution)/shard_map/reduce_scatter | solution.py:131
  209.7 201.3 %all-reduce.6.cloned.1.call-start = ((), (), s32[]{:S(2)}) async-start(), calls=%async_computation.11 | async-start | bytes 819200 | tf_op jit(solution)/shard_map/psum | solution.py:128
  359.8 112.2 %reduce-scatter.7.cloned.1.call-start = ((), (), s32[]{:S(2)}) async-start(), calls=%async_computation.7 | async-start | bytes 4718592 | tf_op jit(solution)/shard_map/reduce_scatter | solution.py:120
  411.0 63.1 %copy-start.18 = (f32[3,3,32,128]{3,2,1,0:T(8,128)S(1)}, f32[3,3,32,128]{3,2,1,0:T(8,128)}, u32[]{:S(2)}) copy-start(f32[3,3,32,128]{3,2,1,0:T(8,128)} %get-tuple-element.46) | copy-start | bytes 442372
  411.0 63.7 %copy-start.19 = (f32[128,256]{1,0:T(8,128)S(1)}, f32[128,256]{1,0:T(8,128)}, u32[]{:S(2)}) copy-start(f32[128,256]{1,0:T(8,128)} %get-tuple-element.47) | copy-start | bytes 393220
  (6 other events, 7.7 us)
Sparse Core Ops, SparseCore 0:
  9.8 59.6 all-gather.2
  72.1 77.0 reduce-scatter.4
  151.3 40.0 all-gather.4
  194.5 75.4 all-reduce.3
  273.1 42.0 reduce-scatter.8
  317.7 41.9 reduce-scatter.10
  362.4 48.5 all-reduce.5
  413.6 58.3 reduce-scatter.6
